TPU v7x, 32 devices: a whole 2x2x4 slice. The times are simulated.
32 devices in a mesh: grp: 4 (over y, core), tile: 8 (over z, x).
Axes of the slice: x: 2, y: 2, z: 4, core: 2. Of those that a mesh axis runs over, the one named last changes fastest.
Arguments:
- material: int32 [6, 1536, 2048], P(None, 'grp', 'tile'), may hold values from 0 to 7
- conduct_table: float32 [8], replicated, may hold values from 1 to 20
- heat_sink: float32 [1536, 2048], P('grp', 'tile'), may hold values from 1 to 10
- heat_source: float32 [6, 1536, 2048], P(None, 'grp', 'tile'), may hold values from -120 to 120
- die_power: float32 [192, 128, 128], P(('grp', 'tile')), may hold values from -60 to 60
- die_conduct: float32 [192], P(('grp', 'tile')), may hold values from 1 to 8
- bond_conductance: float32 [192], P(('grp', 'tile')), may hold values from 0.5 to 4
- tile_place: int32 [192], P(('grp', 'tile')), may hold values from -1 to 191, as said below
Outputs:
- interposer_temp: float32 [6, 1536, 2048], P(None, 'grp', 'tile')
- die_temp: float32 [192, 128, 128], P(('grp', 'tile'))
Inputs may be any that keep to these rules, and one draw needn't show every extreme that they name: `tile_place`: -1 marks an empty slot; the other entries are distinct tile positions; one device holds all 6 of its slots filled and every device at least one.
All inputs are finite; a program needn't handle non-finite values.
Results may differ from a plain program's by a relative error of at most 0.0003.
Values sent between devices are 32-bit elements; how exact they have to be, the bound alone decides.
A program may use at most 192 MiB of HBM per device.

v0:
```python
import jax
import jax.numpy as jnp
from jax import lax
from jax.sharding import PartitionSpec as P

RATIO = 8
NU = 2
NC = 4


relax_weight = 0.8


def extended(block, sides, width):
    for axis, dim in sides:
        count = lax.axis_size(axis)
        forward = [(i, i + 1) for i in range(count - 1)]
        backward = [(target, source) for source, target in forward]
        low = lax.ppermute(
            lax.slice_in_dim(block, block.shape[dim] - width, None, axis=dim), axis, forward
        )
        high = lax.ppermute(lax.slice_in_dim(block, 0, width, axis=dim), axis, backward)
        block = jnp.concatenate([low, block, high], axis=dim)
    return block


def harmonic(lower_side, upper_side):
    total = lower_side + upper_side
    return 2.0 * lower_side * upper_side / jnp.where(total > 0, total, 1.0)


def neighbours(padded):
    return (
        padded[:-2, 1:-1, 1:-1],
        padded[2:, 1:-1, 1:-1],
        padded[1:-1, :-2, 1:-1],
        padded[1:-1, 2:, 1:-1],
        padded[1:-1, 1:-1, :-2],
        padded[1:-1, 1:-1, 2:],
    )


def grid_faces(padded, vertical):
    centre = padded[1:-1, 1:-1, 1:-1]
    scales = (vertical, vertical, 1.0, 1.0, 1.0, 1.0)
    return tuple(
        (
            harmonic(centre, other) * weight_value
            for other, weight_value in zip(neighbours(padded), scales)
        )
    )


def grid_residual(padded, faces, extra, source):
    centre = padded[1:-1, 1:-1, 1:-1]
    flux_sum = extra * centre
    diagonal = extra
    for face, other in zip(faces, neighbours(padded)):
        flux_sum = flux_sum + face * (centre - other)
        diagonal = diagonal + face
    return (source - flux_sum, diagonal)


def grid_sweep(padded, faces, extra, source):
    residual_part, diagonal = grid_residual(padded, faces, extra, source)
    centre = padded[1:-1, 1:-1, 1:-1]
    return centre + relax_weight * residual_part / jnp.where(diagonal > 0, diagonal, 1.0)


def in_block(length, block_size, offset):
    relative = (jnp.arange(length) - offset) % block_size
    return ((relative != 0).astype(jnp.float32), (relative != block_size - 1).astype(jnp.float32))


def die_faces(conduct, block_size, offset):
    lower_x, upper_x = in_block(conduct.shape[-2], block_size, offset)
    lower_y, upper_y = in_block(conduct.shape[-1], block_size, offset)
    return (
        conduct * lower_x[:, None],
        conduct * upper_x[:, None],
        conduct * lower_y[None, :],
        conduct * upper_y[None, :],
    )


def die_residual(field, faces, couple, top_field, source):
    widths = [(0, 0)] * (field.ndim - 2) + [(1, 1), (1, 1)]
    padded = jnp.pad(field, widths)
    views = (
        padded[..., :-2, 1:-1],
        padded[..., 2:, 1:-1],
        padded[..., 1:-1, :-2],
        padded[..., 1:-1, 2:],
    )
    flux_sum = couple * field
    diagonal = couple
    for face, other in zip(faces, views):
        flux_sum = flux_sum + face * (field - other)
        diagonal = diagonal + face
    return (source + couple * top_field - flux_sum, diagonal)


def die_sweep(field, faces, couple, top_field, source):
    residual_part, diagonal = die_residual(field, faces, couple, top_field, source)
    return field + relax_weight * residual_part / jnp.where(diagonal > 0, diagonal, 1.0)


def coarsen(field, factor):
    shape = field.shape
    split = field.reshape(shape[:-2] + (shape[-2] // factor, factor, shape[-1] // factor, factor))
    return split.sum(axis=(-3, -1))


def refine(field, factor):
    return jnp.repeat(jnp.repeat(field, factor, axis=-2), factor, axis=-1)


def on_layers(bottom, top_layer, layer_count):
    middle = jnp.zeros((layer_count - 2,) + bottom.shape, jnp.float32)
    return jnp.concatenate([bottom[None], middle, top_layer[None]], 0)


def cell_conduct(material, conduct_table):
    values = jnp.zeros(material.shape, jnp.float32)
    for kind in range(conduct_table.shape[0]):
        values = values + jnp.where(material == kind, conduct_table[kind], 0.0)
    return values


def blocks_to_field(blocks, blocks_down, blocks_across):
    edge_cells = blocks.shape[-1]
    shaped = blocks.reshape(blocks_down, blocks_across, edge_cells, edge_cells)
    return shaped.transpose(0, 2, 1, 3).reshape(
        blocks_down * edge_cells, blocks_across * edge_cells
    )


def field_to_blocks(field, blocks_down, blocks_across, edge_cells):
    shaped = field.reshape(blocks_down, edge_cells, blocks_across, edge_cells)
    return shaped.transpose(0, 2, 1, 3).reshape(blocks_down * blocks_across, edge_cells, edge_cells)


def layer_pad(field):
    return jnp.pad(field, ((1, 1), (0, 0), (0, 0)))


def per_device(
    material,
    conduct_table,
    heat_sink,
    heat_source,
    die_power,
    die_conduct,
    bond_conductance,
    tile_place,
):
    layer_count, row_count, col_count = material.shape
    slot_count = tile_place.shape[0]
    block_edge = die_power.shape[1]
    coarse_block = block_edge // RATIO
    blocks_down = row_count // block_edge
    blocks_across = col_count // block_edge
    tile_count = lax.axis_size("tile")
    area = float(RATIO * RATIO)
    cell_values = cell_conduct(material, conduct_table)
    cond_pad = extended(cell_values, (("grp", 1), ("tile", 2)), 1)
    fine_faces = grid_faces(layer_pad(cond_pad), 1.0)
    fine_extra = on_layers(heat_sink, jnp.zeros_like(heat_sink), layer_count)

    def fine_padded(field):
        return layer_pad(extended(field, (("grp", 1), ("tile", 2)), 1))

    def smooth(field):
        for repeat_index in range(NU):
            field = grid_sweep(fine_padded(field), fine_faces, fine_extra, heat_source)
        return field

    interposer = smooth(jnp.zeros_like(heat_source))
    fine_resid = grid_residual(fine_padded(interposer), fine_faces, fine_extra, heat_source)[0]
    filled = (tile_place >= 0).astype(jnp.float32)
    ones_block = jnp.ones((1, block_edge, block_edge), jnp.float32)
    slot_faces = die_faces(die_conduct[:, None, None] * ones_block, block_edge, 0)
    slot_couple = bond_conductance[:, None, None] * ones_block
    zero_top = jnp.zeros_like(die_power)
    die_field = jnp.zeros_like(die_power)
    for repeat_index in range(NU):
        die_field = die_sweep(die_field, slot_faces, slot_couple, zero_top, die_power)
    die_resid = (
        die_residual(die_field, slot_faces, slot_couple, zero_top, die_power)[0]
        * filled[:, None, None]
    )
    coarse_rhs = coarsen(fine_resid, RATIO)
    die_coarse = coarsen(die_resid, RATIO).reshape(slot_count, coarse_block * coarse_block)
    span = tile_count * blocks_across
    safe_place = jnp.maximum(tile_place, 0)
    place_row = safe_place // span
    place_col = safe_place % span
    target = place_row // blocks_down * tile_count + place_col // blocks_across
    local_slot = place_row % blocks_down * blocks_across + place_col % blocks_across
    slot_code = jnp.where(tile_place >= 0, target * slot_count + local_slot, -1)
    slot_params = jnp.stack(
        [die_conduct, bond_conductance * area, slot_code.astype(jnp.float32)], axis=1
    )
    all_blocks, all_params = (
        lax.all_gather(die_coarse, ("grp", "tile"), axis=0, tiled=True),
        lax.all_gather(slot_params, ("grp", "tile"), axis=0, tiled=True),
    )
    me_index = lax.axis_index("grp") * tile_count + lax.axis_index("tile")
    wanted = (me_index * slot_count + jnp.arange(slot_count)).astype(jnp.float32)
    chosen = (all_params[:, 2][None, :] == wanted[:, None]).astype(jnp.float32)
    pos_rhs = jnp.dot(chosen, all_blocks, precision=lax.Precision.HIGHEST)
    pos_params = jnp.dot(chosen, all_params[:, :2], precision=lax.Precision.HIGHEST)
    coarse_ones = jnp.ones((1, coarse_block, coarse_block), jnp.float32)
    top_rhs = blocks_to_field(
        pos_rhs.reshape(slot_count, coarse_block, coarse_block), blocks_down, blocks_across
    )
    top_conduct = blocks_to_field(
        pos_params[:, 0][:, None, None] * coarse_ones, blocks_down, blocks_across
    )
    top_couple = blocks_to_field(
        pos_params[:, 1][:, None, None] * coarse_ones, blocks_down, blocks_across
    )
    coarse_k = coarsen(cell_values, RATIO) / area
    coarse_sink = coarsen(heat_sink, RATIO)
    stacked = jnp.concatenate(
        [
            coarse_k,
            coarse_rhs,
            coarse_sink[None],
            top_couple[None],
            top_conduct[None],
            top_rhs[None],
        ],
        0,
    )
    widened = extended(stacked, (("grp", 1), ("tile", 2)), NC)
    wide_k = widened[:layer_count]
    wide_rhs = widened[layer_count : 2 * layer_count]
    wide_sink = widened[2 * layer_count]
    wide_couple = widened[2 * layer_count + 1]
    wide_conduct = widened[2 * layer_count + 2]
    wide_top = widened[2 * layer_count + 3]
    coarse_faces = grid_faces(jnp.pad(wide_k, 1), area)
    top_faces = die_faces(wide_conduct, coarse_block, NC)
    coarse_extra = on_layers(wide_sink, wide_couple, layer_count)
    coarse_error = jnp.zeros_like(wide_rhs)
    top_error = jnp.zeros_like(wide_top)
    for repeat_index in range(NC):
        pull_term = on_layers(jnp.zeros_like(wide_sink), wide_couple * top_error, layer_count)
        next_error = grid_sweep(
            jnp.pad(coarse_error, 1), coarse_faces, coarse_extra, wide_rhs + pull_term
        )
        top_error = die_sweep(top_error, top_faces, wide_couple, coarse_error[-1], wide_top)
        coarse_error = next_error
    coarse_error = coarse_error[:, NC:-NC, NC:-NC]
    top_error = top_error[NC:-NC, NC:-NC]
    owner_blocks = field_to_blocks(top_error, blocks_down, blocks_across, coarse_block).reshape(
        slot_count, coarse_block * coarse_block
    )
    flat_error = lax.psum_scatter(
        jnp.dot(chosen.T, owner_blocks, precision=lax.Precision.HIGHEST),
        ("grp", "tile"),
        scatter_dimension=0,
        tiled=True,
    )
    slot_error = flat_error.reshape(slot_count, coarse_block, coarse_block)
    interposer = smooth(interposer + refine(coarse_error, RATIO))
    die_field = die_field + refine(slot_error, RATIO)
    for repeat_index in range(NU):
        die_field = die_sweep(die_field, slot_faces, slot_couple, zero_top, die_power)
    return (interposer, die_field * filled[:, None, None])


def solution(mesh):
    placed = (
        P(None, "grp", "tile"),
        P(),
        P("grp", "tile"),
        P(None, "grp", "tile"),
        P(("grp", "tile"), None, None),
        P(("grp", "tile")),
        P(("grp", "tile")),
        P(("grp", "tile")),
    )
    return jax.shard_map(
        per_device,
        mesh=mesh,
        in_specs=placed,
        out_specs=(P(None, "grp", "tile"), P(("grp", "tile"), None, None)),
        check_vma=False,
    )
```

profile of v0, /device:TPU:9, one launch (start us, length us, event | category | flops | bytes accessed | tf_op | source)
XLA Modules:
  0.0 681.8 jit_solution(13830456203341756068)
XLA Ops:
  11.5 8.2 %select_add_fusion = f32[6,384,256]{1,2,0:T(8,128)S(1)} fusion(s32[6,384,256]{1,2,0:T(8,128)} %copy.61, f32[]{:T(128)} %bitcast.8, f32[]{:T(128)} %bitcast.7, f32[]{:T(128)} %bitcast.6, f32[]{:T(128)} %bitcast.5, f32[]{:T(128)} %bitcast.4, f32[]{:T(128)} %bitcast.3, f32[]{:T(128)} %bitcast.2, f32[]{:T(128)} %bitcast.1), kind=kLoop, calls=%fused_computation.211 | loop fusion | flops 13565952 | bytes 4718624 | tf_op jit(solution)/shard_map/add | solution.py:126
  32.5 24.6 %reshape.126 = f32[6,48,8,32,8]{4,3,2,1,0:T(8,128)} reshape(f32[6,384,256]{2,1,0:T(8,128)} %copy.87) | data formatting | bytes 4718592 | tf_op jit(solution)/shard_map/reshape | solution.py:110
  57.2 13.7 %reduce_sum.36 = f32[6,48,32]{2,1,0:T(8,128)S(1)} reduce(f32[6,48,8,32,8]{4,3,2,1,0:T(8,128)} %reshape.126, f32[]{:T(128)} %constant.142.clone.1), dimensions={2,4}, to_apply=%region_0.1 | reduce | flops 580608 | bytes 2396164 | tf_op jit(solution)/shard_map/reduce_sum | solution.py:111
  83.9 4.9 reshape.129
  111.0 4.1 collective-permute-start.7
  119.0 4.5 select_maximum_fusion.16
  123.5 12.7 %fusion.10 = (f32[6,384,256]{1,2,0:T(8,128)S(1)}, f32[6,384,256]{1,2,0:T(8,128)}, f32[6,384,256]{1,2,0:T(8,128)}, f32[6,384,256]{1,2,0:T(8,128)}, f32[6,384,256]{1,2,0:T(8,128)}) fusion(f32[6,384,256]{1,2,0:T(8,128)S(1)} %copy-done, f32[6,384,256]{1,2,0:T(8,128)S(1)} %slice.548, f32[6,1,256]{1,2,0:T(8,128)S(1)} %copy-done.31, ...), kind=kLoop, calls=%fused_computation.44 | loop fusion | flops 45416448 | bytes 28766448 | tf_op jit(solution)/shard_map/div | solution.py:67
  140.9 4.8 collective-permute-start.8
  149.6 60.1 %all-gather.1 = f32[32,6,256]{2,1,0:T(8,128)} all-gather(f32[1,6,256]{2,1,0:T(8,128)} %reshape.139), channel_id=1, replica_groups=mesh['grp'=4,'tile'=8] {'grp','tile'}, dimensions={0}, use_global_device_ids=true | all-gather | bytes 202752 | tf_op jit(solution)/shard_map/all_gather | solution.py:205
  209.7 66.1 %all-gather = f32[32,6,3]{1,2,0:T(4,128)S(1)} all-gather(f32[1,6,3]{1,2,0:T(4,128)} %maximum_bitcast_fusion.2), channel_id=1, replica_groups=mesh['grp'=4,'tile'=8] {'grp','tile'}, dimensions={0}, use_global_device_ids=true | all-gather | bytes 2376 | tf_op jit(solution)/shard_map/all_gather | solution.py:206
  289.6 4.2 collective-permute-start.11
  301.0 11.6 %fusion.82 = f32[6,384,256]{1,2,0:T(8,128)S(1)} fusion(f32[6,384,256]{1,2,0:T(8,128)} %copy-done.16, f32[6,384,256]{1,2,0:T(8,128)S(1)} %copy-done.1, f32[6,384,256]{1,2,0:T(8,128)S(1)} %copy-done.15, f32[6,386,1]{1,2,0:T(1,128)S(1)} %collective-permute-done.11, f32[6,1,256]{1,2,0:T(8,128)} %copy.83, f32[6,1,256]{1,2,0:T(8,128)} %copy.82, ...), kind=kLoop, calls=%fused_computation.147 | loop fusion | flops 31850496 | bytes 24029328 | tf_op jit(solution)/shard_map/add | solution.py:67
  317.4 10.9 %collective-permute-start.12 = (f32[6,1,256]{2,1,0:T(1,128)}, f32[6,1,256]{2,1,0:T(1,128)}, u32[]{:S(2)}, u32[]{:S(2)}) collective-permute-start(f32[6,1,256]{2,1,0:T(1,128)} %copy.88), channel_id=1, source_target_pairs={{0,8},{8,16},{16,24},{1,9},{9,17},{17,25},{2,10},{10,18},{18,26},{... | collective-permute-start | bytes 18440 | tf_op jit(solution)/shard_map/ppermute | solution.py:19
  341.1 4.5 collective-permute-start.15
  346.8 5.8 reshape.128
  373.6 9.4 %fusion.62 = f32[6,384,256]{1,2,0:T(8,128)} fusion(f32[6,384,256]{1,2,0:T(8,128)S(1)} %copy-done.2, f32[6,384,256]{1,2,0:T(8,128)} %get-tuple-element.33, f32[6,384,256]{1,2,0:T(8,128)S(1)} %copy-done.6, f32[6,386,1]{1,2,0:T(1,128)} %collective-permute-done.15, f32[6,1,256]{1,2,0:T(8,128)} %copy.91, f32[6,1,256]{1,2,0:T(8,128)} %copy.90, ...), kind=kLoop, calls=%fused_computation.117 | loop fusion | flops 25362432 | bytes 24029328 | tf_op jit(solution)/shard_map/sub | solution.py:61
  386.1 24.6 %reshape.127 = f32[6,48,8,32,8]{4,3,2,1,0:T(8,128)} reshape(f32[6,384,256]{2,1,0:T(8,128)} %copy.95) | data formatting | bytes 4718592 | tf_op jit(solution)/shard_map/reshape | solution.py:110
  410.7 14.3 %reduce_sum.37 = f32[6,48,32]{2,1,0:T(8,128)} reduce(f32[6,48,8,32,8]{4,3,2,1,0:T(8,128)} %reshape.127, f32[]{:T(128)} %constant.142.clone.1), dimensions={2,4}, to_apply=%region_1.2 | reduce | flops 580608 | bytes 2396164 | tf_op jit(solution)/shard_map/reduce_sum | solution.py:111
  428.9 4.2 collective-permute-start.16
  440.5 4.3 collective-permute-start.19
  444.8 13.9 %collective-permute-done.18 = f32[16,56,4]{2,1,0:T(8,128)S(1)} collective-permute-done((f32[16,56,4]{2,1,0:T(8,128)S(1)}, f32[16,56,4]{2,1,0:T(8,128)S(1)}, u32[]{:S(2)}, u32[]{:S(2)}) %collective-permute-start.18) | collective-permute-done | bytes 14368 | tf_op jit(solution)/shard_map/ppermute | solution.py:19
  471.3 57.3 %fusion = f32[8,256]{1,0:T(8,128)S(1)} fusion(f32[192,256]{1,0:T(8,128)} %fusion.342), kind=kCustom, calls=%all-reduce-scatter | all-reduce-scatter fusion | flops 65537 | bytes 204800
  531.0 6.0 collective-permute-start.29
  548.7 6.7 collective-permute-start.20
  563.1 7.4 %collective-permute-start.30 = (f32[8,256]{1,0:T(8,128)S(1)}, f32[8,256]{1,0:T(8,128)}, u32[]{:S(2)}, u32[]{:S(2)}) collective-permute-start(f32[8,256]{1,0:T(8,128)S(1)} %fusion), channel_id=1, source_target_pairs={{0,3},{1,4},{2,5},{3,6},{4,7},{5,8},{6,9},{7,10},{8,11},{9,12},{10... | collective-permute-start | bytes 24584
  574.8 4.6 collective-permute-start.32
  587.2 4.2 collective-permute-start.23
  592.6 12.4 %concatenate.180 = f32[70,256]{1,0:T(8,128)} concatenate(f32[6,256]{1,0:T(8,128)} %collective-permute-done.35, f32[8,256]{1,0:T(8,128)} %collective-permute-done.34, f32[8,256]{1,0:T(8,128)} %copy-done.54, f32[8,256]{1,0:T(8,128)} %copy-done.53, f32[8,256]{1,0:T(8,128)} %collective-permute-done.31, f32[8,256]{1,0:T(8,128)} %collective-permute-done.30, ...), dimensions={0} | concatenate | bytes 143360
  616.0 11.2 %fusion.45 = f32[6,384,256]{1,2,0:T(8,128)S(1)} fusion(f32[6,384,256]{1,2,0:T(8,128)} %copy-done.17, f32[6,384,256]{1,2,0:T(8,128)S(1)} %copy-done.3, f32[6,384,256]{1,2,0:T(8,128)} %get-tuple-element.33, f32[6,386,1]{1,2,0:T(1,128)} %collective-permute-done.23, f32[6,1,256]{1,2,0:T(8,128)} %copy.104, f32[6,1,256]{1,2,0:T(8,128)S(1)} %copy-done.30, ...), kind=kLoop, calls=%fused_computation.90 | loop fusion | flops 31850496 | bytes 24029328 | tf_op jit(solution)/shard_map/add | solution.py:67
  635.9 5.2 collective-permute-start.25
  651.7 4.3 collective-permute-start.27
  664.5 13.8 %fusion.25 = f32[6,384,256]{1,2,0:T(8,128)} fusion(f32[6,384,256]{1,2,0:T(8,128)} %copy-done.18, f32[6,384,256]{1,2,0:T(8,128)S(1)} %copy-done.4, f32[6,384,256]{1,2,0:T(8,128)} %get-tuple-element.33, f32[6,386,1]{1,2,0:T(1,128)} %collective-permute-done.27, f32[6,1,256]{1,2,0:T(8,128)} %copy.111, f32[6,1,256]{1,2,0:T(8,128)} %copy.110, ...), kind=kLoop, calls=%fused_computation.60 | loop fusion | flops 31850496 | bytes 24029328 | tf_op jit(solution)/shard_map/add | solution.py:67
  (297 shorter events, 235.0 us)
Async XLA Ops:
  1.2 102.1 %collective-permute-start.4 = (f32[6,1,256]{2,1,0:T(1,128)}, f32[6,1,256]{2,1,0:T(1,128)}, u32[]{:S(2)}, u32[]{:S(2)}) collective-permute-start(f32[6,1,256]{2,1,0:T(1,128)} %broadcast.341), channel_id=1, source_target_pairs={{0,8},{8,16},{16,24},{1,9},{9,17},{17,25},{2,10},{10,18},{18,26},{... | collective-permute-start | bytes 18440 | tf_op jit(solution)/shard_map/ppermute | solution.py:19
  4.9 100.3 %collective-permute-start.5 = (f32[6,1,256]{2,1,0:T(1,128)}, f32[6,1,256]{2,1,0:T(1,128)}, u32[]{:S(2)}, u32[]{:S(2)}) collective-permute-start(f32[6,1,256]{2,1,0:T(1,128)} %broadcast.341), channel_id=1, source_target_pairs={{8,0},{16,8},{24,16},{9,1},{17,9},{25,17},{10,2},{18,10},{26,18},{... | collective-permute-start | bytes 18440 | tf_op jit(solution)/shard_map/ppermute | solution.py:22
  22.8 69.9 %collective-permute-start = (f32[6,1,256]{2,1,0:T(1,128)}, f32[6,1,256]{2,1,0:T(1,128)}, u32[]{:S(2)}, u32[]{:S(2)}) collective-permute-start(f32[6,1,256]{2,1,0:T(1,128)} %copy.69), channel_id=1, source_target_pairs={{0,8},{8,16},{16,24},{1,9},{9,17},{17,25},{2,10},{10,18},{18,26},{... | collective-permute-start | bytes 18440 | tf_op jit(solution)/shard_map/ppermute | solution.py:19
  27.3 66.4 %collective-permute-start.1 = (f32[6,1,256]{2,1,0:T(1,128)}, f32[6,1,256]{2,1,0:T(1,128)}, u32[]{:S(2)}, u32[]{:S(2)}) collective-permute-start(f32[6,1,256]{2,1,0:T(1,128)} %copy.70), channel_id=1, source_target_pairs={{8,0},{16,8},{24,16},{9,1},{17,9},{25,17},{10,2},{18,10},{26,18},{... | collective-permute-start | bytes 18440 | tf_op jit(solution)/shard_map/ppermute | solution.py:22
  97.1 18.0 %collective-permute-start.2 = (f32[6,386,1]{1,2,0:T(1,128)}, f32[6,386,1]{1,2,0:T(1,128)}, u32[]{:S(2)}, u32[]{:S(2)}) collective-permute-start(f32[6,386,1]{1,2,0:T(1,128)} %get-tuple-element.42), channel_id=1, source_target_pairs={{0,1},{1,2},{2,3},{3,4},{4,5},{5,6},{6,7},{8,9},{9,10},{10,11},{11... | collective-permute-start | bytes 27800 | tf_op jit(solution)/shard_map/ppermute | solution.py:19
  100.3 14.9 %collective-permute-start.3 = (f32[6,386,1]{1,2,0:T(1,128)}, f32[6,386,1]{1,2,0:T(1,128)}, u32[]{:S(2)}, u32[]{:S(2)}) collective-permute-start(f32[6,386,1]{1,2,0:T(1,128)} %get-tuple-element.43), channel_id=1, source_target_pairs={{1,0},{2,1},{3,2},{4,3},{5,4},{6,5},{7,6},{9,8},{10,9},{11,10},{12... | collective-permute-start | bytes 27800 | tf_op jit(solution)/shard_map/ppermute | solution.py:22
  108.6 10.4 %collective-permute-start.6 = (f32[6,386,1]{1,2,0:T(1,128)S(1)}, f32[6,386,1]{1,2,0:T(1,128)S(1)}, u32[]{:S(2)}, u32[]{:S(2)}) collective-permute-start(f32[6,386,1]{1,2,0:T(1,128)S(1)} %get-tuple-element.44), channel_id=1, source_target_pairs={{0,1},{1,2},{2,3},{3,4},{4,5},{5,6},{6,7},{8,9},{9,10},{10,11},{11... | collective-permute-start | bytes 27800 | tf_op jit(solution)/shard_map/ppermute | solution.py:19
  111.0 8.1 %collective-permute-start.7 = (f32[6,386,1]{1,2,0:T(1,128)S(1)}, f32[6,386,1]{1,2,0:T(1,128)S(1)}, u32[]{:S(2)}, u32[]{:S(2)}) collective-permute-start(f32[6,386,1]{1,2,0:T(1,128)S(1)} %get-tuple-element.45), channel_id=1, source_target_pairs={{1,0},{2,1},{3,2},{4,3},{5,4},{6,5},{7,6},{9,8},{10,9},{11,10},{12... | collective-permute-start | bytes 27800 | tf_op jit(solution)/shard_map/ppermute | solution.py:22
  140.9 139.9 %collective-permute-start.8 = (f32[6,1,256]{2,1,0:T(1,128)}, f32[6,1,256]{2,1,0:T(1,128)}, u32[]{:S(2)}, u32[]{:S(2)}) collective-permute-start(f32[6,1,256]{2,1,0:T(1,128)} %copy.80), channel_id=1, source_target_pairs={{0,8},{8,16},{16,24},{1,9},{9,17},{17,25},{2,10},{10,18},{18,26},{... | collective-permute-start | bytes 18440 | tf_op jit(solution)/shard_map/ppermute | solution.py:19
  147.7 135.1 %collective-permute-start.9 = (f32[6,1,256]{2,1,0:T(1,128)}, f32[6,1,256]{2,1,0:T(1,128)}, u32[]{:S(2)}, u32[]{:S(2)}) collective-permute-start(f32[6,1,256]{2,1,0:T(1,128)} %copy.81), channel_id=1, source_target_pairs={{8,0},{16,8},{24,16},{9,1},{17,9},{25,17},{10,2},{18,10},{26,18},{... | collective-permute-start | bytes 18440 | tf_op jit(solution)/shard_map/ppermute | solution.py:22
  285.9 9.7 %collective-permute-start.10 = (f32[6,386,1]{1,2,0:T(1,128)S(1)}, f32[6,386,1]{1,2,0:T(1,128)S(1)}, u32[]{:S(2)}, u32[]{:S(2)}) collective-permute-start(f32[6,386,1]{1,2,0:T(1,128)S(1)} %get-tuple-element.40), channel_id=1, source_target_pairs={{0,1},{1,2},{2,3},{3,4},{4,5},{5,6},{6,7},{8,9},{9,10},{10,11},{11... | collective-permute-start | bytes 27800 | tf_op jit(solution)/shard_map/ppermute | solution.py:19
  317.4 16.3 %collective-permute-start.12 = (f32[6,1,256]{2,1,0:T(1,128)}, f32[6,1,256]{2,1,0:T(1,128)}, u32[]{:S(2)}, u32[]{:S(2)}) collective-permute-start(f32[6,1,256]{2,1,0:T(1,128)} %copy.88), channel_id=1, source_target_pairs={{0,8},{8,16},{16,24},{1,9},{9,17},{17,25},{2,10},{10,18},{18,26},{... | collective-permute-start | bytes 18440 | tf_op jit(solution)/shard_map/ppermute | solution.py:19
  339.2 29.8 %collective-permute-start.14 = (f32[6,386,1]{1,2,0:T(1,128)}, f32[6,386,1]{1,2,0:T(1,128)}, u32[]{:S(2)}, u32[]{:S(2)}) collective-permute-start(f32[6,386,1]{1,2,0:T(1,128)} %get-tuple-element.38), channel_id=1, source_target_pairs={{0,1},{1,2},{2,3},{3,4},{4,5},{5,6},{6,7},{8,9},{9,10},{10,11},{11... | collective-permute-start | bytes 27800 | tf_op jit(solution)/shard_map/ppermute | solution.py:19
  341.1 27.9 %collective-permute-start.15 = (f32[6,386,1]{1,2,0:T(1,128)}, f32[6,386,1]{1,2,0:T(1,128)}, u32[]{:S(2)}, u32[]{:S(2)}) collective-permute-start(f32[6,386,1]{1,2,0:T(1,128)} %get-tuple-element.39), channel_id=1, source_target_pairs={{1,0},{2,1},{3,2},{4,3},{5,4},{6,5},{7,6},{9,8},{10,9},{11,10},{12... | collective-permute-start | bytes 27800 | tf_op jit(solution)/shard_map/ppermute | solution.py:22
  438.6 20.1 %collective-permute-start.18 = (f32[16,56,4]{2,1,0:T(8,128)S(1)}, f32[16,56,4]{2,1,0:T(8,128)S(1)}, u32[]{:S(2)}, u32[]{:S(2)}) collective-permute-start(f32[16,56,4]{2,1,0:T(8,128)S(1)} %get-tuple-element.58), channel_id=1, source_target_pairs={{0,1},{1,2},{2,3},{3,4},{4,5},{5,6},{6,7},{8,9},{9,10},{10,11},{11... | collective-permute-start | bytes 43016 | tf_op jit(solution)/shard_map/ppermute | solution.py:19
  440.5 21.5 %collective-permute-start.19 = (f32[16,56,4]{2,1,0:T(8,128)S(1)}, f32[16,56,4]{2,1,0:T(8,128)S(1)}, u32[]{:S(2)}, u32[]{:S(2)}) collective-permute-start(f32[16,56,4]{2,1,0:T(8,128)S(1)} %get-tuple-element.59), channel_id=1, source_target_pairs={{1,0},{2,1},{3,2},{4,3},{5,4},{6,5},{7,6},{9,8},{10,9},{11,10},{12... | collective-permute-start | bytes 43016 | tf_op jit(solution)/shard_map/ppermute | solution.py:22
  528.6 50.8 %collective-permute-start.28 = (f32[8,256]{1,0:T(8,128)S(1)}, f32[8,256]{1,0:T(8,128)}, u32[]{:S(2)}, u32[]{:S(2)}) collective-permute-start(f32[8,256]{1,0:T(8,128)S(1)} %fusion), channel_id=1, source_target_pairs={{0,1},{1,2},{2,3},{3,4},{4,5},{5,6},{6,7},{7,8},{8,9},{9,10},{10,1... | collective-permute-start | bytes 24584
  531.0 50.3 %collective-permute-start.29 = (f32[8,256]{1,0:T(8,128)S(1)}, f32[8,256]{1,0:T(8,128)}, u32[]{:S(2)}, u32[]{:S(2)}) collective-permute-start(f32[8,256]{1,0:T(8,128)S(1)} %fusion), channel_id=1, source_target_pairs={{0,2},{1,3},{2,4},{3,5},{4,6},{5,7},{6,8},{7,9},{8,10},{9,11},{10,... | collective-permute-start | bytes 24584
  548.7 14.3 %collective-permute-start.20 = (f32[6,1,256]{2,1,0:T(1,128)S(1)}, f32[6,1,256]{2,1,0:T(1,128)S(1)}, u32[]{:S(2)}, u32[]{:S(2)}) collective-permute-start(f32[6,1,256]{2,1,0:T(1,128)S(1)} %copy.101), channel_id=1, source_target_pairs={{0,8},{8,16},{16,24},{1,9},{9,17},{17,25},{2,10},{10,18},{18,26},{... | collective-permute-start | bytes 18440 | tf_op jit(solution)/shard_map/ppermute | solution.py:19
  556.9 14.8 %collective-permute-start.21 = (f32[6,1,256]{2,1,0:T(1,128)S(1)}, f32[6,1,256]{2,1,0:T(1,128)S(1)}, u32[]{:S(2)}, u32[]{:S(2)}) collective-permute-start(f32[6,1,256]{2,1,0:T(1,128)S(1)} %copy.102), channel_id=1, source_target_pairs={{8,0},{16,8},{24,16},{9,1},{17,9},{25,17},{10,2},{18,10},{26,18},{... | collective-permute-start | bytes 18440 | tf_op jit(solution)/shard_map/ppermute | solution.py:22
  559.4 15.4 %collective-permute-start.35 = (f32[6,256]{1,0:T(8,128)}, f32[6,256]{1,0:T(8,128)}, u32[]{:S(2)}, u32[]{:S(2)}) collective-permute-start(f32[6,256]{1,0:T(8,128)} %slice.751), channel_id=1, source_target_pairs={{0,8},{1,9},{2,10},{3,11},{4,12},{5,13},{6,14},{7,15},{8,16},{9,17... | collective-permute-start | bytes 18440
  563.1 22.2 %collective-permute-start.30 = (f32[8,256]{1,0:T(8,128)S(1)}, f32[8,256]{1,0:T(8,128)}, u32[]{:S(2)}, u32[]{:S(2)}) collective-permute-start(f32[8,256]{1,0:T(8,128)S(1)} %fusion), channel_id=1, source_target_pairs={{0,3},{1,4},{2,5},{3,6},{4,7},{5,8},{6,9},{7,10},{8,11},{9,12},{10... | collective-permute-start | bytes 24584
  571.7 15.5 %collective-permute-start.31 = (f32[8,256]{1,0:T(8,128)S(1)}, f32[8,256]{1,0:T(8,128)}, u32[]{:S(2)}, u32[]{:S(2)}) collective-permute-start(f32[8,256]{1,0:T(8,128)S(1)} %fusion), channel_id=1, source_target_pairs={{0,4},{1,5},{2,6},{3,7},{4,8},{5,9},{6,10},{7,11},{8,12},{9,13},{1... | collective-permute-start | bytes 24584
  574.8 16.6 %collective-permute-start.32 = (f32[8,256]{1,0:T(8,128)S(1)}, f32[8,256]{1,0:T(8,128)S(1)}, u32[]{:S(2)}, u32[]{:S(2)}) collective-permute-start(f32[8,256]{1,0:T(8,128)S(1)} %fusion), channel_id=1, source_target_pairs={{0,5},{1,6},{2,7},{3,8},{4,9},{5,10},{6,11},{7,12},{8,13},{9,14},{... | collective-permute-start | bytes 24584
  579.4 12.0 %collective-permute-start.33 = (f32[8,256]{1,0:T(8,128)S(1)}, f32[8,256]{1,0:T(8,128)S(1)}, u32[]{:S(2)}, u32[]{:S(2)}) collective-permute-start(f32[8,256]{1,0:T(8,128)S(1)} %fusion), channel_id=1, source_target_pairs={{0,6},{1,7},{2,8},{3,9},{4,10},{5,11},{6,12},{7,13},{8,14},{9,15},... | collective-permute-start | bytes 24584
  581.3 11.3 %collective-permute-start.34 = (f32[8,256]{1,0:T(8,128)S(1)}, f32[8,256]{1,0:T(8,128)}, u32[]{:S(2)}, u32[]{:S(2)}) collective-permute-start(f32[8,256]{1,0:T(8,128)S(1)} %fusion), channel_id=1, source_target_pairs={{0,7},{1,8},{2,9},{3,10},{4,11},{5,12},{6,13},{7,14},{8,15},{9,16}... | collective-permute-start | bytes 24584
  585.2 26.2 %collective-permute-start.22 = (f32[6,386,1]{1,2,0:T(1,128)}, f32[6,386,1]{1,2,0:T(1,128)}, u32[]{:S(2)}, u32[]{:S(2)}) collective-permute-start(f32[6,386,1]{1,2,0:T(1,128)} %get-tuple-element.36), channel_id=1, source_target_pairs={{0,1},{1,2},{2,3},{3,4},{4,5},{5,6},{6,7},{8,9},{9,10},{10,11},{11... | collective-permute-start | bytes 27800 | tf_op jit(solution)/shard_map/ppermute | solution.py:19
  587.2 24.3 %collective-permute-start.23 = (f32[6,386,1]{1,2,0:T(1,128)}, f32[6,386,1]{1,2,0:T(1,128)}, u32[]{:S(2)}, u32[]{:S(2)}) collective-permute-start(f32[6,386,1]{1,2,0:T(1,128)} %get-tuple-element.37), channel_id=1, source_target_pairs={{1,0},{2,1},{3,2},{4,3},{5,4},{6,5},{7,6},{9,8},{10,9},{11,10},{12... | collective-permute-start | bytes 27800 | tf_op jit(solution)/shard_map/ppermute | solution.py:22
  632.0 12.3 %collective-permute-start.24 = (f32[6,1,256]{2,1,0:T(1,128)}, f32[6,1,256]{2,1,0:T(1,128)}, u32[]{:S(2)}, u32[]{:S(2)}) collective-permute-start(f32[6,1,256]{2,1,0:T(1,128)} %copy.108), channel_id=1, source_target_pairs={{0,8},{8,16},{16,24},{1,9},{9,17},{17,25},{2,10},{10,18},{18,26},{... | collective-permute-start | bytes 18440 | tf_op jit(solution)/shard_map/ppermute | solution.py:19
  635.9 10.3 %collective-permute-start.25 = (f32[6,1,256]{2,1,0:T(1,128)}, f32[6,1,256]{2,1,0:T(1,128)}, u32[]{:S(2)}, u32[]{:S(2)}) collective-permute-start(f32[6,1,256]{2,1,0:T(1,128)} %copy.109), channel_id=1, source_target_pairs={{8,0},{16,8},{24,16},{9,1},{17,9},{25,17},{10,2},{18,10},{26,18},{... | collective-permute-start | bytes 18440 | tf_op jit(solution)/shard_map/ppermute | solution.py:22
  649.8 10.1 %collective-permute-start.26 = (f32[6,386,1]{1,2,0:T(1,128)}, f32[6,386,1]{1,2,0:T(1,128)}, u32[]{:S(2)}, u32[]{:S(2)}) collective-permute-start(f32[6,386,1]{1,2,0:T(1,128)} %get-tuple-element.34), channel_id=1, source_target_pairs={{0,1},{1,2},{2,3},{3,4},{4,5},{5,6},{6,7},{8,9},{9,10},{10,11},{11... | collective-permute-start | bytes 27800 | tf_op jit(solution)/shard_map/ppermute | solution.py:19
  651.7 8.2 %collective-permute-start.27 = (f32[6,386,1]{1,2,0:T(1,128)}, f32[6,386,1]{1,2,0:T(1,128)}, u32[]{:S(2)}, u32[]{:S(2)}) collective-permute-start(f32[6,386,1]{1,2,0:T(1,128)} %get-tuple-element.35), channel_id=1, source_target_pairs={{1,0},{2,1},{3,2},{4,3},{5,4},{6,5},{7,6},{9,8},{10,9},{11,10},{12... | collective-permute-start | bytes 27800 | tf_op jit(solution)/shard_map/ppermute | solution.py:22
  (60 other events, 1078.4 us)
where the time goes:
time: 692 us; the launch traced here: 682 us
  blocking collectives  184 us (27%)
  local copies, waits for them, and re-layouts  183 us (26%)
  other arithmetic  158 us (23%)
  starting transfers between devices  128 us (18%)
  waiting for transfers between devices  21.8 us (3%)
    all_gather x1, blocking collectives, per_device(): lax.all_gather(slot_params, ('grp', 'tile'), axis=0, tiled=True)  66.1 us
    all_gather x1, blocking collectives, per_device(): lax.all_gather(die_coarse, ('grp', 'tile'), axis=0, tiled=True)  60.1 us
    reshape x4, local copies, waits for them, and re-layouts, coarsen(): field.reshape(shape[:-2] + (shape[-2] // factor, factor, shape[-1] // fac...  60 us
    unnamed x1, blocking collectives  57.3 us
    ppermute x14, starting transfers between devices, extended(): lax.ppermute(lax.slice_in_dim(block, block.shape[dim] - width, None, axis...  52.8 us
    ppermute x14, starting transfers between devices, extended(): lax.ppermute(lax.slice_in_dim(block, 0, width, axis=dim), axis, backward)  45.4 us
    unnamed x128, local copies, waits for them, and re-layouts  44.2 us
    add x6, other arithmetic, grid_sweep(): centre + relax_weight * residual_part / jnp.where(diagonal > 0, diagonal,...  38.7 us
  transfers between devices with their start and end apart: 36, of which 4 were waited for; matrix products, arithmetic and copies ran while one was open for 26% of the time, Pallas kernels for 0%

commit v1 on v0

v1 whole, which is shorter than its diff:
```python
import functools
import jax
import jax.numpy as jnp
from jax import lax
from jax.experimental import pallas as pl
from jax.experimental.pallas import tpu as pltpu
from jax.sharding import PartitionSpec as P

RATIO = 8
NU = 2
NC = 4
RELAX = 0.8
HALO = 4
TOP = 16
LANES = 128
MESH = pl.DeviceIdType.MESH
HIGHEST = lax.Precision.HIGHEST
DIRECTIONS = ((-1, 0), (1, 0), (0, -1), (0, 1), (-1, -1), (-1, 1), (1, -1), (1, 1))


def inverse(x):
    r = pl.reciprocal(x, approx=True)
    return r * (2.0 - x * r)


def harmonic(a, b):
    total = a + b
    return 2.0 * a * b * inverse(jnp.where(total > 0, total, 1.0))


def guarded_weight(d):
    return RELAX * inverse(jnp.where(d > 0, d, 1.0))


def iota(shape, dim):
    return lax.broadcasted_iota(jnp.int32, shape, dim)


def shift(x, amount, axis):
    return pltpu.roll(x, amount % x.shape[axis], axis)


def rows_at(ref, l, r, offset):
    if offset < 0:
        return ref.at[l, pl.ds(pl.multiple_of(r - 8, 8), 16), :][8 + offset : 16 + offset, :]
    return ref.at[l, pl.ds(r, 16), :][offset : 8 + offset, :]


def dot(a, b):
    return jnp.dot(a, b, precision=HIGHEST, preferred_element_type=jnp.float32)


def kernel(
    grp_count,
    tile_count,
    material,
    table,
    heat_sink,
    source,
    die_power,
    die_conduct,
    bond,
    place,
    out,
    die_out,
    field,
    zx,
    zy,
    zz,
    diag,
    weight,
    ua,
    ub,
    packed,
    turned,
    from_side,
    from_corner,
    sums,
    rough,
    rough_side,
    rough_row,
    rough_corner,
    dies,
    die_message,
    all_dies,
    die_fix,
    all_fixes,
    wide,
    solved,
    spread,
    send_sem,
    recv_sem,
    gather_send,
    gather_recv,
):
    layers, rows, cols = material.shape
    slots, edge, _ = die_power.shape
    cell = edge // RATIO
    down, across = rows // edge, cols // edge
    crows, ccols = rows // RATIO, cols // RATIO
    width = cols + LANES
    height = rows + 2 * TOP
    n_fields = 2 * layers + 1
    area = float(RATIO * RATIO)
    per = LANES // ccols
    count = grp_count * tile_count
    g = lax.axis_index("grp")
    t = lax.axis_index("tile")
    me = g * tile_count + t

    def peer(offset):
        other = lax.rem(me + offset, count)
        return other, (other // tile_count, lax.rem(other, tile_count))

    def exists(dy, dx):
        ok = jnp.bool_(True)
        if dy:
            ok = jnp.logical_and(ok, g > 0 if dy < 0 else g < grp_count - 1)
        if dx:
            ok = jnp.logical_and(ok, t > 0 if dx < 0 else t < tile_count - 1)
        return ok

    field[:, 0:TOP, :] = jnp.zeros((n_fields, TOP, width), jnp.float32)
    field[:, height - TOP : height, :] = jnp.zeros((n_fields, TOP, width), jnp.float32)
    from_side[...] = jnp.zeros_like(from_side)
    from_corner[...] = jnp.zeros_like(from_corner)
    rough_side[...] = jnp.zeros_like(rough_side)
    rough_row[...] = jnp.zeros_like(rough_row)
    rough_corner[...] = jnp.zeros_like(rough_corner)
    zx[:, 0:8, :] = jnp.zeros((layers, 8, width), jnp.float32)

    barrier = pltpu.get_barrier_semaphore()

    @pl.loop(1, count)
    def _(offset):
        pl.semaphore_signal(barrier, inc=1, device_id=peer(offset)[1], device_id_type=MESH)

    lane8 = iota((8, LANES), 1)

    @pl.loop(0, rows // 8)
    def _(i):
        r = pl.multiple_of(i * 8, 8)
        edges = jnp.zeros((8, LANES), jnp.float32)
        for f in range(n_fields):
            if f < layers:
                kind = material[f, pl.ds(r, 8), :]
                values = [jnp.full((8, cols), table[m], jnp.float32) for m in range(table.shape[0])]
                bit = 1
                while len(values) > 1:
                    odd = (kind & bit) != 0
                    values = [
                        jnp.where(odd, values[m + 1], values[m]) if m + 1 < len(values) else values[m]
                        for m in range(0, len(values), 2)
                    ]
                    bit *= 2
                x = values[0]
            elif f < 2 * layers:
                x = source[f - layers, pl.ds(r, 8), :]
            else:
                x = heat_sink[pl.ds(r, 8), :]
            field[f, pl.ds(TOP + r, 8), 0:cols] = x
            if f < layers or f == 2 * layers:
                s = f if f < layers else layers
                sums[s, pl.ds(i, 1), :] = jnp.sum(x, axis=0, keepdims=True)
            right = shift(x[:, cols - LANES :], HALO + HALO * f, 1)
            left = shift(x[:, :LANES], 64 + HALO * f, 1)
            in_right = (lane8 >= HALO * f) & (lane8 < HALO * (f + 1))
            in_left = (lane8 >= 64 + HALO * f) & (lane8 < 64 + HALO * (f + 1))
            edges = jnp.where(in_right, right, jnp.where(in_left, left, edges))
        packed[pl.ds(r, 8), :] = edges

    turned[...] = packed[...].T

    pl.semaphore_wait(barrier, count - 1)

    depth = from_side.shape[1]

    def halo_copy(k):
        dy, dx = DIRECTIONS[k]
        if dx == 0:
            src = field.at[:, pl.ds(TOP if dy < 0 else height - TOP - 8, 8), pl.ds(0, cols)]
            dst = field.at[:, pl.ds(height - TOP if dy < 0 else TOP - 8, 8), pl.ds(0, cols)]
        elif dy == 0:
            src = turned.at[pl.ds(0 if dx > 0 else 64, depth), :]
            dst = from_side.at[0 if dx > 0 else 1]
        else:
            src = packed.at[pl.ds(0 if dy < 0 else rows - 8, 8), :]
            dst = from_corner.at[k - 4]
        return pltpu.make_async_remote_copy(
            src_ref=src, dst_ref=dst, send_sem=send_sem.at[k], recv_sem=recv_sem.at[k],
            device_id=(g + dy, t + dx), device_id_type=MESH,
        )

    def rough_copy(k, phase):
        dy, dx = DIRECTIONS[k]
        half = pl.ds(2 * phase, 2)
        if dy == 0:
            src = rough.at[half]
            dst = rough_side.at[k - 2, half]
        else:
            src = rough.at[half, pl.ds(0 if dy < 0 else crows - 8, 8), :]
            dst = (rough_row.at[k, half] if dx == 0 else rough_corner.at[k - 4, half])
        s = 8 * (phase + 1) + k
        return pltpu.make_async_remote_copy(
            src_ref=src, dst_ref=dst, send_sem=send_sem.at[s], recv_sem=recv_sem.at[s],
            device_id=(g + dy, t + dx), device_id_type=MESH,
        )

    def start_all(make):
        for k, (dy, dx) in enumerate(DIRECTIONS):
            pl.when(exists(dy, dx))(lambda k=k: make(k).start())

    def wait_all_recv(make):
        for k, (dy, dx) in enumerate(DIRECTIONS):
            pl.when(exists(-dy, -dx))(lambda k=k: make(k).wait_recv())

    def wait_all_send(make):
        for k, (dy, dx) in enumerate(DIRECTIONS):
            pl.when(exists(dy, dx))(lambda k=k: make(k).wait_send())

    start_all(halo_copy)

    srow, scol = iota((edge, edge), 0), iota((edge, edge), 1)
    one, none = jnp.float32(1.0), jnp.float32(0.0)
    sides = (
        jnp.where(srow > 0, one, none) + jnp.where(srow < edge - 1, one, none)
        + jnp.where(scol > 0, one, none) + jnp.where(scol < edge - 1, one, none)
    )

    def around(v):
        return (
            jnp.where(srow > 0, shift(v, 1, 0), 0.0)
            + jnp.where(srow < edge - 1, shift(v, -1, 0), 0.0)
            + jnp.where(scol > 0, shift(v, 1, 1), 0.0)
            + jnp.where(scol < edge - 1, shift(v, -1, 1), 0.0)
        )

    rows_in = (iota((cell, edge), 0) == iota((cell, edge), 1) // RATIO).astype(jnp.float32)
    message = jnp.zeros((cell, LANES), jnp.float32)
    row_m = iota((8, LANES), 0)
    params = jnp.full((8, LANES), -1.0, jnp.float32)
    for s in range(slots):
        c, b = die_conduct[s], bond[s]
        live = jnp.where(place[s] >= 0, 1.0, 0.0)
        p = die_power[s]
        d = c * sides + b
        wt = guarded_weight(d)
        v = wt * p
        v = (1.0 - RELAX) * v + wt * (p + c * around(v))
        dies[s] = v
        resid = live * (p + c * around(v) - d * v)
        cols_in = (
            iota((edge, LANES), 0) // RATIO + cell * s == iota((edge, LANES), 1)
        ).astype(jnp.float32)
        message = message + dot(dot(rows_in, resid), cols_in)
        mine = lane8 // cell == s
        value = jnp.where(
            row_m == 0, c, jnp.where(row_m == 1, b * area, place[s].astype(jnp.float32))
        )
        params = jnp.where(mine, value, params)
    die_message[0:cell, :] = message
    die_message[cell : cell + 8, :] = params
    all_dies[me] = die_message[...]

    def gather_copy(phase, other, slot, where):
        src, dst = (die_message, all_dies) if phase == 0 else (die_fix, all_fixes)
        return pltpu.make_async_remote_copy(
            src_ref=src, dst_ref=dst.at[slot],
            send_sem=gather_send.at[phase, other], recv_sem=gather_recv.at[phase, slot],
            device_id=where, device_id_type=MESH,
        )

    def gather_start(phase):
        @pl.loop(1, count)
        def _(offset):
            other, where = peer(offset)
            gather_copy(phase, other, me, where).start()

    def gather_wait(phase):
        @pl.loop(1, count)
        def _(offset):
            other, where = peer(offset)
            gather_copy(phase, other, other, where).wait()

    gather_start(0)

    def gathered(first, total, tile):
        result = jnp.zeros((crows, LANES), jnp.float32)
        for q in range(per):
            f = tile * per + q
            if f < total:
                pick = (
                    iota((cols, LANES), 0) // RATIO + q * ccols == iota((cols, LANES), 1)
                ).astype(jnp.float32)
                result = result + dot(sums[first + f], pick)
        return result

    for tile in range(2):
        rough[tile] = gathered(0, layers + 1, tile)
    start_all(lambda k: rough_copy(k, 0))

    wait_all_recv(halo_copy)
    filler = jnp.zeros((64 - depth, rows), jnp.float32)
    arrived = jnp.concatenate([from_side[0], filler, from_side[1], filler], axis=0)
    ua[0, TOP : height - TOP, cols:width] = arrived.T
    upper = jnp.where(lane8 < 64, from_corner[3], from_corner[2])
    lower = jnp.where(lane8 < 64, from_corner[1], from_corner[0])
    ua[0, TOP - 8 : TOP, cols:width] = upper
    ua[0, height - TOP : height - TOP + 8, cols:width] = lower

    @pl.loop(1, height // 8 - 1)
    def _(i):
        r = pl.multiple_of(i * 8, 8)
        x = ua[0, pl.ds(r, 8), cols:width]
        for f in range(n_fields):
            left = shift(x, -HALO * (f + 1), 1)
            right = shift(x, -64 - HALO * f, 1)
            field[f, pl.ds(r, 8), cols:width] = jnp.where(
                lane8 >= LANES - HALO, left, jnp.where(lane8 < HALO, right, 0.0)
            )

    @pl.loop(1, height // 8 - 1)
    def _(i):
        r = pl.multiple_of(i * 8, 8)
        ks = [field[l, pl.ds(r, 8), :] for l in range(layers)]
        below = None
        for l in range(layers):
            k = ks[l]
            fx = harmonic(k, rows_at(field, l, r, 1))
            fy = harmonic(k, shift(k, -1, 1))
            zx[l, pl.ds(r, 8), :] = fx
            zy[l, pl.ds(r, 8), :] = fy
            d = fx + rows_at(zx, l, r, -1) + fy + shift(fy, 1, 1)
            if l == 0:
                d = d + field[2 * layers, pl.ds(r, 8), :]
            else:
                d = d + below
            if l < layers - 1:
                below = harmonic(k, ks[l + 1])
                zz[l, pl.ds(r, 8), :] = below
                d = d + below
            diag[l, pl.ds(r, 8), :] = d
            wt = guarded_weight(d)
            weight[l, pl.ds(r, 8), :] = wt
            ua[l, pl.ds(r, 8), :] = wt * field[layers + l, pl.ds(r, 8), :]

    def pulled(u, r, l, us):
        centre = us[l]
        fx = zx[l, pl.ds(r, 8), :]
        fy = zy[l, pl.ds(r, 8), :]
        total = field[layers + l, pl.ds(r, 8), :]
        total = total + fx * rows_at(u, l, r, 1)
        total = total + rows_at(zx, l, r, -1) * rows_at(u, l, r, -1)
        total = total + fy * shift(centre, -1, 1) + shift(fy * centre, 1, 1)
        if l > 0:
            total = total + zz[l - 1, pl.ds(r, 8), :] * us[l - 1]
        if l < layers - 1:
            total = total + zz[l, pl.ds(r, 8), :] * us[l + 1]
        return total

    def sweep(u, store, first, last):
        @pl.loop(first, last)
        def _(i):
            r = pl.multiple_of(i * 8, 8)
            us = [u[l, pl.ds(r, 8), :] for l in range(layers)]
            for l in range(layers):
                total = pulled(u, r, l, us)
                new = (1.0 - RELAX) * us[l] + weight[l, pl.ds(r, 8), :] * total
                store(l, r, new)

    def into(ref):
        def store(l, r, new):
            ref[l, pl.ds(r, 8), :] = new

        return store

    sweep(ua, into(ub), 1, height // 8 - 1)

    @pl.loop(0, crows)
    def _(i):
        r = pl.multiple_of(i * 8 + TOP, 8)
        us = [ub[l, pl.ds(r, 8), :] for l in range(layers)]
        for l in range(layers):
            resid = pulled(ub, r, l, us) - diag[l, pl.ds(r, 8), :] * us[l]
            sums[layers + 1 + l, pl.ds(i, 1), :] = jnp.sum(resid[:, :cols], axis=0, keepdims=True)

    for tile in range(2):
        rough[2 + tile] = gathered(layers + 1, layers, tile)
    start_all(lambda k: rough_copy(k, 1))

    gather_wait(0)
    span = tile_count * across
    chigh = crows + 16
    parts = cell + 8
    spots = [(a, b) for a in range(-1, down + 1) for b in range(-1, across + 1)]
    wanted = []
    for a, b in spots:
        pr, pc = g * down + a, t * across + b
        inside = (pr >= 0) & (pr < grp_count * down) & (pc >= 0) & (pc < span)
        wanted.append(jnp.where(inside, pr * span + pc, -2).astype(jnp.float32))

    for lo in range(0, len(spots), across + 2):

        def add(d, acc, lo=lo):
            block = all_dies[d]
            where = block[cell + 2 : cell + 3, :]
            return tuple(
                a + jnp.where(where == wanted[lo + j], block, 0.0) for j, a in enumerate(acc)
            )

        acc = lax.fori_loop(
            0, count, add, tuple(jnp.zeros((parts, LANES), jnp.float32) for _ in range(across + 2))
        )
        lane_p = iota((parts, LANES), 1)
        line = jnp.zeros((parts, LANES), jnp.float32)
        for j in range(across + 2):
            x = acc[j]
            step = LANES // 2
            while step >= cell:
                x = x + shift(x, step, 1)
                step //= 2
            line = jnp.where(lane_p // cell == j, x, line)
        line = shift(line, 8 - cell, 1)
        a = lo // (across + 2) - 1
        if a == -1:
            first, size, off = 0, 8, cell - 8
        elif a == down:
            first, size, off = 8 + crows, 8, 0
        else:
            first, size, off = 8 + a * cell, cell, 0
        n = 2 * layers + 1
        wide[n, first : first + size, :] = line[off : off + size]
        wide[n + 1, first : first + size, :] = jnp.broadcast_to(
            line[cell : cell + 1], (size, LANES)
        )
        wide[n + 2, first : first + size, :] = jnp.broadcast_to(
            line[cell + 1 : cell + 2], (size, LANES)
        )

    for phase in range(2):
        wait_all_recv(lambda k: rough_copy(k, phase))
        for f in range(layers + 1 if phase == 0 else layers):
            tile, q = 2 * phase + f // per, f % per
            target = f if phase == 0 else layers + 1 + f

            def joined(left, middle, right, size):
                lane = iota((size, LANES), 1)
                x = shift(middle, 8 - ccols * q, 1)
                x = jnp.where((lane >= 8) & (lane < 8 + ccols), x, 0.0)
                x = jnp.where(lane < 8, shift(left, 8 - ccols - ccols * q, 1), x)
                return jnp.where(
                    (lane >= 8 + ccols) & (lane < 16 + ccols),
                    shift(right, 8 + ccols - ccols * q, 1),
                    x,
                )

            wide[target, 8 : 8 + crows, :] = joined(
                rough_side[1, tile], rough[tile], rough_side[0, tile], crows
            )
            wide[target, 0:8, :] = joined(
                rough_corner[3, tile], rough_row[1, tile], rough_corner[2, tile], 8
            )
            wide[target, 8 + crows : chigh, :] = joined(
                rough_corner[1, tile], rough_row[0, tile], rough_corner[0, tile], 8
            )

    kc = [wide[l] * (1.0 / area) for l in range(layers)]
    cx = [harmonic(k, shift(k, -1, 0)) for k in kc]
    cy = [harmonic(k, shift(k, -1, 1)) for k in kc]
    cz = [harmonic(kc[l], kc[l + 1]) * area for l in range(layers - 1)]
    top_rhs, top_c, top_b = (wide[2 * layers + 1 + j] for j in range(3))
    weights = []
    for l in range(layers):
        d = cx[l] + shift(cx[l], 1, 0) + cy[l] + shift(cy[l], 1, 1)
        if l == 0:
            d = d + wide[layers]
        else:
            d = d + cz[l - 1]
        d = d + (cz[l] if l < layers - 1 else top_b)
        weights.append(guarded_weight(d))
    crow = (iota((chigh, LANES), 0) + (cell - 8)) % cell
    ccol = (iota((chigh, LANES), 1) + (cell - 8)) % cell
    low_x, high_x = crow != 0, crow != cell - 1
    low_y, high_y = ccol != 0, ccol != cell - 1
    near = sum(jnp.where(m, one, none) for m in (low_x, high_x, low_y, high_y))
    top_d = top_c * near + top_b
    top_w = guarded_weight(top_d)
    errors = [weights[l] * wide[layers + 1 + l] for l in range(layers)]
    top = top_w * top_rhs
    for _ in range(NC - 1):
        new = []
        for l in range(layers):
            e = errors[l]
            total = wide[layers + 1 + l]
            total = total + cx[l] * shift(e, -1, 0) + shift(cx[l] * e, 1, 0)
            total = total + cy[l] * shift(e, -1, 1) + shift(cy[l] * e, 1, 1)
            if l > 0:
                total = total + cz[l - 1] * errors[l - 1]
            total = total + (cz[l] * errors[l + 1] if l < layers - 1 else top_b * top)
            new.append((1.0 - RELAX) * e + weights[l] * total)
        nearby = (
            jnp.where(low_x, shift(top, 1, 0), 0.0)
            + jnp.where(high_x, shift(top, -1, 0), 0.0)
            + jnp.where(low_y, shift(top, 1, 1), 0.0)
            + jnp.where(high_y, shift(top, -1, 1), 0.0)
        )
        top = top + top_w * (
            top_rhs + top_b * errors[layers - 1] + top_c * nearby - top_d * top
        )
        errors = new
    for l in range(layers):
        solved[l] = errors[l]

    lane_c = iota((cell, LANES), 1)
    fix = jnp.zeros((cell, LANES), jnp.float32)
    for a in range(down):
        piece = shift(top[8 + a * cell : 8 + (a + 1) * cell], a * ccols - 8, 1)
        fix = jnp.where(lane_c // ccols == a, piece, fix)
    die_fix[...] = fix
    all_fixes[me] = die_fix[...]
    gather_start(1)

    column = iota((LANES, width), 1)
    source_lane = jnp.where(column < cols + LANES // 2, 8 + column // RATIO, 7)
    pick = (iota((LANES, width), 0) == source_lane).astype(jnp.float32)
    for l in range(layers):
        spread[l] = dot(solved[l], pick)

    @pl.loop(1, height // 8 - 1)
    def _(i):
        r = pl.multiple_of(i * 8, 8)
        for l in range(layers):
            ub[l, pl.ds(r, 8), :] = ub[l, pl.ds(r, 8), :] + spread[l, pl.ds(i + 6, 1), :]

    sweep(ub, into(ua), 1, height // 8 - 1)

    def finish(l, r, new):
        out[l, pl.ds(r - TOP, 8), :] = new[:, :cols]

    sweep(ua, finish, TOP // 8, (height - TOP) // 8)

    gather_wait(1)
    codes = []
    for s in range(slots):
        spot = jnp.maximum(place[s], 0)
        pr, pc = spot // span, lax.rem(spot, span)
        target = (pr // down) * tile_count + pc // across
        local = lax.rem(pr, down) * across + lax.rem(pc, across)
        codes.append(jnp.where(place[s] >= 0, target * 8 + local, -1))
    group = lane_c // cell

    def collect(d, acc):
        block = all_fixes[d]
        code = group + d * 8
        return tuple(a + jnp.where(code == codes[s], block, 0.0) for s, a in enumerate(acc))

    fixes = lax.fori_loop(
        0, count, collect, tuple(jnp.zeros((cell, LANES), jnp.float32) for _ in range(slots))
    )
    rows_out = (iota((edge, cell), 0) // RATIO == iota((edge, cell), 1)).astype(jnp.float32)
    cols_out = (iota((LANES, edge), 0) == iota((LANES, edge), 1) // RATIO).astype(jnp.float32)
    for s in range(slots):
        x = fixes[s]
        step = LANES // 2
        while step >= cell:
            x = x + shift(x, step, 1)
            step //= 2
        c, b = die_conduct[s], bond[s]
        live = jnp.where(place[s] >= 0, 1.0, 0.0)
        p = die_power[s]
        wt = guarded_weight(c * sides + b)
        v = dies[s] + live * dot(rows_out, dot(x, cols_out))
        for _ in range(NU):
            v = (1.0 - RELAX) * v + wt * (p + c * around(v))
        die_out[s] = live * v

    wait_all_send(halo_copy)
    for phase in range(2):
        wait_all_send(lambda k: rough_copy(k, phase))


def per_device(grp_count, tile_count, *args):
    material, die_power = args[0], args[4]
    layers, rows, cols = material.shape
    slots, edge, _ = die_power.shape
    cell = edge // RATIO
    crows = rows // RATIO
    width, height = cols + LANES, rows + 2 * TOP
    count = grp_count * tile_count
    n_fields = 2 * layers + 1
    depth = -(-n_fields * HALO // 8) * 8
    vmem = pl.BlockSpec(memory_space=pltpu.VMEM)
    smem = pl.BlockSpec(memory_space=pltpu.SMEM)
    f32 = jnp.float32

    def scratch(*shape):
        return pltpu.VMEM(shape, f32)

    grid = (layers, height, width)
    return pl.pallas_call(
        functools.partial(kernel, grp_count, tile_count),
        out_shape=(
            jax.ShapeDtypeStruct((layers, rows, cols), f32),
            jax.ShapeDtypeStruct((slots, edge, edge), f32),
        ),
        in_specs=[vmem, smem, vmem, vmem, vmem, smem, smem, smem],
        out_specs=(vmem, vmem),
        scratch_shapes=[
            scratch(n_fields, height, width),
            scratch(*grid),
            scratch(*grid),
            scratch(layers - 1, height, width),
            scratch(*grid),
            scratch(*grid),
            scratch(*grid),
            scratch(*grid),
            scratch(rows, LANES),
            scratch(LANES, rows),
            scratch(2, depth, rows),
            scratch(4, 8, LANES),
            scratch(n_fields, crows, cols),
            scratch(4, crows, LANES),
            scratch(2, 4, crows, LANES),
            scratch(2, 4, 8, LANES),
            scratch(4, 4, 8, LANES),
            scratch(slots, edge, edge),
            scratch(cell + 8, LANES),
            scratch(count, cell + 8, LANES),
            scratch(cell, LANES),
            scratch(count, cell, LANES),
            scratch(n_fields + 3, crows + 16, LANES),
            scratch(layers, crows + 16, LANES),
            scratch(layers, crows + 16, width),
            pltpu.SemaphoreType.DMA((24,)),
            pltpu.SemaphoreType.DMA((24,)),
            pltpu.SemaphoreType.DMA((2, count)),
            pltpu.SemaphoreType.DMA((2, count)),
        ],
        compiler_params=pltpu.CompilerParams(
            collective_id=0, has_side_effects=True, vmem_limit_bytes=60 * 1024 * 1024
        ),
    )(*args)


def solution(mesh):
    placed = (
        P(None, "grp", "tile"),
        P(),
        P("grp", "tile"),
        P(None, "grp", "tile"),
        P(("grp", "tile"), None, None),
        P(("grp", "tile")),
        P(("grp", "tile")),
        P(("grp", "tile")),
    )
    return jax.shard_map(
        functools.partial(per_device, mesh.shape["grp"], mesh.shape["tile"]),
        mesh=mesh,
        in_specs=placed,
        out_specs=(P(None, "grp", "tile"), P(("grp", "tile"), None, None)),
        check_vma=False,
    )
```

time: 692 us -> 77.8 us (0.11); the launches traced: 682 us -> 77.6 us
  blocking collectives: 184 us -> 0 us
  local copies, waits for them, and re-layouts: 183 us -> 4.16 us
  other arithmetic: 158 us -> 0 us
  starting transfers between devices: 128 us -> 0 us
  Pallas kernels: 0 us -> 72.8 us
  waiting for transfers between devices: 21.8 us -> 0 us
    all_gather x2 -> x0, blocking collectives: 126 us -> none  [the longest x1 66.1 us: per_device(): lax.all_gather(slot_params, ('grp', 'tile'), axis=0, tiled=True)]
    ppermute x28 -> x0, starting transfers between devices: 98.2 us -> none  [the longest x14 52.8 us: extended(): lax.ppermute(lax.slice_in_dim(block, block.shape[dim] - width, None, axis...]
    pallas_call x0 -> x1, Pallas kernels: none -> 72.8 us  [per_device(): pl.pallas_call(functools.partial(kernel, grp_count, tile_count), out_shap...]
    reshape x10 -> x0, local copies, waits for them, and re-layouts: 67.5 us -> none  [the longest x4 60 us: coarsen(): field.reshape(shape[:-2] + (shape[-2] // factor, factor, shape[-1] // fac...]
    unnamed x1 -> x0, blocking collectives: 57.3 us -> none
    add x14 -> x0, other arithmetic: 57 us -> none  [the longest x6 38.7 us: grid_sweep(): centre + relax_weight * residual_part / jnp.where(diagonal > 0, diagonal,...]
    unnamed x128 -> x4, local copies, waits for them, and re-layouts: 44.2 us -> 4.16 us
    reduce_sum x4 -> x0, other arithmetic: 35.2 us -> none  [coarsen(): return split.sum(axis=(-3, -1))]
  transfers between devices with their start and end apart: 36 -> 0, of which waited for: 4 -> 0; matrix products, arithmetic and copies ran while one was open for 26% -> 0% of each run, Pallas kernels for 0% -> 0%
where the time goes in v1:
time: 77.8 us; the launch traced here: 77.6 us
  Pallas kernels  72.8 us (94%)
  local copies, waits for them, and re-layouts  4.16 us (5%)
    pallas_call x1, Pallas kernels, per_device(): pl.pallas_call(functools.partial(kernel, grp_count, tile_count), out_shap...  72.8 us
    unnamed x4, local copies, waits for them, and re-layouts  4.16 us

profile of v1, /device:TPU:9, one launch (start us, length us, event | category | flops | bytes accessed | tf_op | source)
XLA Modules:
  0.0 77.6 jit_solution(4670182836392053628)
XLA Ops:
  0.6 72.8 %shard_map.95 = (f32[6,384,256]{2,1,0:T(8,128)}, f32[6,128,128]{2,1,0:T(8,128)}) custom-call(s32[6,384,256]{2,1,0:T(8,128)} %material.1, f32[8]{0:T(128)} %table.1, f32[384,256]{1,0:T(8,128)} %heat_sink.1, f32[6,384,256]{2,1,0:T(8,128)} %source.1, f32[6,128,128]{2,1,0:T(8,128)} %die_power.1, f32[6]{0:T(128)} %die_conduct.1, f32[6]{0:T(128)} %bond.1, s32[6]{0:T(128)} %place.1), custom_call_target="tpu_custom_call" | custom-call | tf_op jit(solution)/shard_map/pallas_call | solution.py:600
  73.4 0.0 copy-start
  73.4 3.4 %copy.12 = f32[6,384,256]{2,1,0:T(8,128)} copy(f32[6,384,256]{2,1,0:T(8,128)} %get-tuple-element.4) | data formatting | bytes 4718592
  76.8 0.0 copy-done
  76.8 0.7 copy.13
Async XLA Ops:
  73.4 3.4 %copy-start = (f32[6,128,128]{2,1,0:T(8,128)S(1)}, f32[6,128,128]{2,1,0:T(8,128)}, u32[]{:S(2)}) copy-start(f32[6,128,128]{2,1,0:T(8,128)} %get-tuple-element.5) | copy-start | bytes 1179652

commit v2 on v1

--- a/solution.py
+++ b/solution.py
@@ -44,6 +44,20 @@
     if offset < 0:
         return ref.at[l, pl.ds(pl.multiple_of(r - 8, 8), 16), :][8 + offset : 16 + offset, :]
     return ref.at[l, pl.ds(r, 16), :][offset : 8 + offset, :]
+
+
+def row_sums(fields):
+    shape = fields[0].shape
+    row = lax.broadcasted_iota(jnp.int32, shape, 0)
+    xs = list(fields) + [jnp.zeros(shape, jnp.float32)] * (8 - len(fields))
+
+    def merge(x, y, start, run):
+        first = ((row - start + 8) % 8) % (2 * run) < run
+        return jnp.where(first, x, y) + shift(jnp.where(first, y, x), -run, 0)
+
+    z = [merge(xs[j], xs[j + 4], j, 4) for j in range(4)]
+    y = [merge(z[j], z[j + 2], j, 2) for j in range(2)]
+    return merge(y[0], y[1], 0, 1)
 
 
 def dot(a, b):
@@ -76,6 +90,8 @@
     from_side,
     from_corner,
     sums,
+    folded,
+    arrived,
     rough,
     rough_side,
     rough_row,
@@ -141,6 +157,7 @@
     def _(i):
         r = pl.multiple_of(i * 8, 8)
         edges = jnp.zeros((8, LANES), jnp.float32)
+        summed = []
         for f in range(n_fields):
             if f < layers:
                 kind = material[f, pl.ds(r, 8), :]
@@ -160,14 +177,14 @@
                 x = heat_sink[pl.ds(r, 8), :]
             field[f, pl.ds(TOP + r, 8), 0:cols] = x
             if f < layers or f == 2 * layers:
-                s = f if f < layers else layers
-                sums[s, pl.ds(i, 1), :] = jnp.sum(x, axis=0, keepdims=True)
+                summed.append(x)
             right = shift(x[:, cols - LANES :], HALO + HALO * f, 1)
             left = shift(x[:, :LANES], 64 + HALO * f, 1)
             in_right = (lane8 >= HALO * f) & (lane8 < HALO * (f + 1))
             in_left = (lane8 >= 64 + HALO * f) & (lane8 < 64 + HALO * (f + 1))
             edges = jnp.where(in_right, right, jnp.where(in_left, left, edges))
         packed[pl.ds(r, 8), :] = edges
+        sums[pl.ds(r, 8), :] = row_sums(summed)
 
     turned[...] = packed[...].T
 
@@ -284,44 +301,57 @@
 
     gather_start(0)
 
-    def gathered(first, total, tile):
-        result = jnp.zeros((crows, LANES), jnp.float32)
-        for q in range(per):
-            f = tile * per + q
-            if f < total:
-                pick = (
-                    iota((cols, LANES), 0) // RATIO + q * ccols == iota((cols, LANES), 1)
-                ).astype(jnp.float32)
-                result = result + dot(sums[first + f], pick)
-        return result
-
-    for tile in range(2):
-        rough[tile] = gathered(0, layers + 1, tile)
+    def gathered(total, first_tile):
+        pick = (iota((cols, LANES), 0) // RATIO == iota((cols, LANES), 1)).astype(jnp.float32)
+        folded[...] = dot(sums[...], pick)
+        for tile in range(2):
+            result = jnp.zeros((crows, LANES), jnp.float32)
+            for q in range(per):
+                f = tile * per + q
+                if f < total:
+                    result = result + shift(folded[pl.ds(f, crows, stride=8), :], q * ccols, 1)
+            rough[first_tile + tile] = result
+
+    gathered(layers + 1, 0)
     start_all(lambda k: rough_copy(k, 0))
 
     wait_all_recv(halo_copy)
-    filler = jnp.zeros((64 - depth, rows), jnp.float32)
-    arrived = jnp.concatenate([from_side[0], filler, from_side[1], filler], axis=0)
-    ua[0, TOP : height - TOP, cols:width] = arrived.T
-    upper = jnp.where(lane8 < 64, from_corner[3], from_corner[2])
-    lower = jnp.where(lane8 < 64, from_corner[1], from_corner[0])
-    ua[0, TOP - 8 : TOP, cols:width] = upper
-    ua[0, height - TOP : height - TOP + 8, cols:width] = lower
+    pairs = []
+    for f in range(n_fields):
+        pairs.append(from_side[0, HALO * f : HALO * (f + 1), :])
+        pairs.append(from_side[1, HALO * f : HALO * (f + 1), :])
+    pairs.append(jnp.zeros((LANES - 2 * HALO * n_fields, rows), jnp.float32))
+    arrived[TOP : height - TOP, :] = jnp.concatenate(pairs, axis=0).T
+
+    def corner(x, y):
+        tile = jnp.zeros((8, LANES), jnp.float32)
+        for f in range(n_fields):
+            at = lane8 - 2 * HALO * f
+            tile = jnp.where((at >= 0) & (at < HALO), shift(x, HALO * f, 1), tile)
+            tile = jnp.where(
+                (at >= HALO) & (at < 2 * HALO), shift(y, HALO * f + HALO - 64, 1), tile
+            )
+        return tile
+
+    arrived[0 : TOP - 8, :] = jnp.zeros((TOP - 8, LANES), jnp.float32)
+    arrived[TOP - 8 : TOP, :] = corner(from_corner[3], from_corner[2])
+    arrived[height - TOP : height - TOP + 8, :] = corner(from_corner[1], from_corner[0])
+    arrived[height - TOP + 8 : height, :] = jnp.zeros((TOP - 8, LANES), jnp.float32)
+    in_halo = (lane8 < HALO) | (lane8 >= LANES - HALO)
+
+    def unpack(r):
+        x = arrived[pl.ds(r, 8), :]
+        for f in range(n_fields):
+            field[f, pl.ds(r, 8), cols:width] = jnp.where(
+                in_halo, shift(x, -HALO * (2 * f + 1), 1), 0.0
+            )
+
+    unpack(8)
 
     @pl.loop(1, height // 8 - 1)
     def _(i):
         r = pl.multiple_of(i * 8, 8)
-        x = ua[0, pl.ds(r, 8), cols:width]
-        for f in range(n_fields):
-            left = shift(x, -HALO * (f + 1), 1)
-            right = shift(x, -64 - HALO * f, 1)
-            field[f, pl.ds(r, 8), cols:width] = jnp.where(
-                lane8 >= LANES - HALO, left, jnp.where(lane8 < HALO, right, 0.0)
-            )
-
-    @pl.loop(1, height // 8 - 1)
-    def _(i):
-        r = pl.multiple_of(i * 8, 8)
+        unpack(pl.multiple_of(r + 8, 8))
         ks = [field[l, pl.ds(r, 8), :] for l in range(layers)]
         below = None
         for l in range(layers):
@@ -380,12 +410,13 @@
     def _(i):
         r = pl.multiple_of(i * 8 + TOP, 8)
         us = [ub[l, pl.ds(r, 8), :] for l in range(layers)]
+        resids = []
         for l in range(layers):
             resid = pulled(ub, r, l, us) - diag[l, pl.ds(r, 8), :] * us[l]
-            sums[layers + 1 + l, pl.ds(i, 1), :] = jnp.sum(resid[:, :cols], axis=0, keepdims=True)
-
-    for tile in range(2):
-        rough[2 + tile] = gathered(layers + 1, layers, tile)
+            resids.append(resid[:, :cols])
+        sums[pl.ds(pl.multiple_of(i * 8, 8), 8), :] = row_sums(resids)
+
+    gathered(layers, 2)
     start_all(lambda k: rough_copy(k, 1))
 
     gather_wait(0)
@@ -618,7 +649,9 @@
             scratch(LANES, rows),
             scratch(2, depth, rows),
             scratch(4, 8, LANES),
-            scratch(n_fields, crows, cols),
+            scratch(rows, cols),
+            scratch(rows, LANES),
+            scratch(height, LANES),
             scratch(4, crows, LANES),
             scratch(2, 4, crows, LANES),
             scratch(2, 4, 8, LANES),

time: 77.8 us -> 77.2 us (level)
  no operation moved by 1% of the time
where the time goes in v2:
time: 77.2 us; the launch traced here: 77 us
  Pallas kernels  72.2 us (94%)
  local copies, waits for them, and re-layouts  4.16 us (5%)
    pallas_call x1, Pallas kernels, per_device(): pl.pallas_call(functools.partial(kernel, grp_count, tile_count), out_shap...  72.2 us
    unnamed x4, local copies, waits for them, and re-layouts  4.16 us

profile of v2, /device:TPU:9, one launch (start us, length us, event | category | flops | bytes accessed | tf_op | source)
XLA Modules:
  0.0 77.0 jit_solution(520599357282264739)
XLA Ops:
  0.6 72.2 %shard_map.95 = (f32[6,384,256]{2,1,0:T(8,128)}, f32[6,128,128]{2,1,0:T(8,128)}) custom-call(s32[6,384,256]{2,1,0:T(8,128)} %material.1, f32[8]{0:T(128)} %table.1, f32[384,256]{1,0:T(8,128)} %heat_sink.1, f32[6,384,256]{2,1,0:T(8,128)} %source.1, f32[6,128,128]{2,1,0:T(8,128)} %die_power.1, f32[6]{0:T(128)} %die_conduct.1, f32[6]{0:T(128)} %bond.1, s32[6]{0:T(128)} %place.1), custom_call_target="tpu_custom_call" | custom-call | tf_op jit(solution)/shard_map/pallas_call | solution.py:631
  72.8 0.0 copy-start
  72.8 3.4 %copy.12 = f32[6,384,256]{2,1,0:T(8,128)} copy(f32[6,384,256]{2,1,0:T(8,128)} %get-tuple-element.4) | data formatting | bytes 4718592
  76.3 0.0 copy-done
  76.3 0.7 copy.13
Async XLA Ops:
  72.8 3.4 %copy-start = (f32[6,128,128]{2,1,0:T(8,128)S(1)}, f32[6,128,128]{2,1,0:T(8,128)}, u32[]{:S(2)}) copy-start(f32[6,128,128]{2,1,0:T(8,128)} %get-tuple-element.5) | copy-start | bytes 1179652

commit v3 on v2

--- a/solution.py
+++ b/solution.py
@@ -670,7 +670,7 @@
             pltpu.SemaphoreType.DMA((2, count)),
         ],
         compiler_params=pltpu.CompilerParams(
-            collective_id=0, has_side_effects=True, vmem_limit_bytes=60 * 1024 * 1024
+            collective_id=0, has_side_effects=True, vmem_limit_bytes=47 * 1024 * 1024
         ),
     )(*args)
 

time: 77.2 us -> 79.2 us (1.026)
  local copies, waits for them, and re-layouts: 4.16 us -> 8.42 us
  Pallas kernels: 72.2 us -> 69.7 us
    unnamed x4 -> x16, local copies, waits for them, and re-layouts: 4.16 us -> 8.42 us
    pallas_call x1, Pallas kernels: 72.2 us -> 69.7 us  [per_device(): pl.pallas_call(functools.partial(kernel, grp_count, tile_count), out_shap...]
where the time goes in v3:
time: 79.2 us; the launch traced here: 78.8 us
  Pallas kernels  69.7 us (88%)
  local copies, waits for them, and re-layouts  8.42 us (11%)
    pallas_call x1, Pallas kernels, per_device(): pl.pallas_call(functools.partial(kernel, grp_count, tile_count), out_shap...  69.7 us
    unnamed x16, local copies, waits for them, and re-layouts  8.42 us

profile of v3, /device:TPU:9, one launch (start us, length us, event | category | flops | bytes accessed | tf_op | source)
XLA Modules:
  0.0 78.8 jit_solution(2188440079616777392)
XLA Ops:
  0.6 0.0 copy-start
  0.6 1.7 %copy-done = s32[6,384,256]{2,1,0:T(8,128)S(1)} copy-done((s32[6,384,256]{2,1,0:T(8,128)S(1)}, s32[6,384,256]{2,1,0:T(8,128)}, u32[]{:S(2)}) %copy-start) | copy-done | bytes 2359320
  2.3 0.0 copy-start.1
  2.3 1.0 %copy-done.1 = f32[384,256]{1,0:T(8,128)S(1)} copy-done((f32[384,256]{1,0:T(8,128)S(1)}, f32[384,256]{1,0:T(8,128)}, u32[]{:S(2)}) %copy-start.1) | copy-done | bytes 393240
  3.3 0.0 copy-start.2
  3.3 1.0 %copy-done.2 = f32[6,128,128]{2,1,0:T(8,128)S(1)} copy-done((f32[6,128,128]{2,1,0:T(8,128)S(1)}, f32[6,128,128]{2,1,0:T(8,128)}, u32[]{:S(2)}) %copy-start.2) | copy-done | bytes 393240
  4.3 0.0 copy-start.3
  4.3 0.7 copy-done.3
  4.9 0.0 copy-start.4
  4.9 0.7 copy-done.4
  5.6 0.0 copy-start.5
  5.6 0.7 copy-done.5
  6.3 0.0 copy-start.6
  6.3 0.7 copy-done.6
  6.9 69.7 %shard_map.95 = (f32[6,384,256]{2,1,0:T(8,128)S(1)}, f32[6,128,128]{2,1,0:T(8,128)S(1)}) custom-call(s32[6,384,256]{2,1,0:T(8,128)S(1)} %copy-done, f32[8]{0:T(128)S(1)} %copy-done.3, f32[384,256]{1,0:T(8,128)S(1)} %copy-done.1, f32[6,384,256]{2,1,0:T(8,128)} %source.1, f32[6,128,128]{2,1,0:T(8,128)S(1)} %copy-done.2, f32[6]{0:T(128)S(1)} %copy-done.4, ...), custom_call_target="tpu_custom_call" | custom-call | tf_op jit(solution)/shard_map/pallas_call | solution.py:631
  76.6 1.4 %copy.12 = f32[6,384,256]{2,1,0:T(8,128)} copy(f32[6,384,256]{2,1,0:T(8,128)S(1)} %get-tuple-element.4) | data formatting | bytes 4718592
  78.1 0.7 copy.13
Async XLA Ops:
  0.6 1.7 %copy-start = (s32[6,384,256]{2,1,0:T(8,128)S(1)}, s32[6,384,256]{2,1,0:T(8,128)}, u32[]{:S(2)}) copy-start(s32[6,384,256]{2,1,0:T(8,128)} %material.1) | copy-start | bytes 7077892
  2.3 1.0 %copy-start.1 = (f32[384,256]{1,0:T(8,128)S(1)}, f32[384,256]{1,0:T(8,128)}, u32[]{:S(2)}) copy-start(f32[384,256]{1,0:T(8,128)} %heat_sink.1) | copy-start | bytes 1179652
  3.3 1.0 %copy-start.2 = (f32[6,128,128]{2,1,0:T(8,128)S(1)}, f32[6,128,128]{2,1,0:T(8,128)}, u32[]{:S(2)}) copy-start(f32[6,128,128]{2,1,0:T(8,128)} %die_power.1) | copy-start | bytes 1179652
  4.3 0.7 copy-start.3
  4.9 0.7 copy-start.4
  5.6 0.7 copy-start.5
  6.3 0.7 copy-start.6
